TPU v7x, 256 devices: a whole 4x4x8 slice. The times are simulated.
256 devices in a mesh: section: 4 (over y), depth: 4 (over z_hi), grid: 16 (over z_lo, x, core).
Axes of the slice: x: 4, y: 4, z: 8 (z_hi: 4, z_lo: 2; z = z_hi * 2 + z_lo), core: 2. Of those that a mesh axis runs over, the one named last changes fastest.
Arguments:
- section_input: bfloat16 [4, 1024, 6144], P('section', 'depth', 'grid'), may hold values from -24 to 24
- cotangent: bfloat16 [4, 1024, 6144], P('section', 'depth', 'grid'), may hold values from -1.796875 to 1.796875
- projections: bfloat16 [4, 6144, 4, 4096], P('section', 'depth', None, 'grid'), may hold values from -0.25 to 0.25
- norm_gain: bfloat16 [4, 6144], P('section', 'grid'), may hold values from 0.099609375 to 1.8984375
- head_gains: bfloat16 [4, 2, 32, 128], P('section', None, 'grid'), may hold values from 0.099609375 to 1.8984375
Outputs:
- next_branch: bfloat16 [4, 1024, 6144], P('section', 'depth', 'grid')
- returned_grad: bfloat16 [4, 1024, 6144], P('section', 'depth', 'grid')
- projection_grad: bfloat16 [4, 6144, 4, 4096], P('section', 'depth', None, 'grid')
- norm_gain_grad: float32 [4, 6144], P('section', 'grid')
- head_gain_grad: float32 [4, 2, 32, 128], P('section', None, 'grid')
All inputs are finite; a program needn't handle non-finite values.
Results may differ from a plain program's by a relative error of at most 0.025.
Values may be sent and summed in bfloat16 or wider, within the bound.
A program may use at most 128 MiB of HBM per device.

v0:
```python
import jax
import jax.numpy as jnp
from jax import lax
from jax.sharding import PartitionSpec as P

SEQ = 256


epsilon = 1e-06


def shifted(value, axis, by):
    peers = lax.axis_size(axis)
    return lax.ppermute(value, axis, [(i, (i + by) % peers) for i in range(peers)])


def normalize(values):
    centre = jnp.mean(values, axis=-1, keepdims=True)
    second = jnp.mean(values * values, axis=-1, keepdims=True)
    reciprocal = lax.rsqrt(second - centre * centre + epsilon)
    return ((values - centre) * reciprocal, reciprocal, centre)


def normalize_back(upstream, normed, reciprocal, gain_row):
    scaled = upstream * gain_row
    first_mean = jnp.mean(scaled, axis=-1, keepdims=True)
    second_mean = jnp.mean(scaled * normed, axis=-1, keepdims=True)
    return reciprocal * (scaled - first_mean - normed * second_mean)


def local(section_input, cotangent, projections, norm_gain, head_gains):
    gathered = (
        lax.all_gather(section_input, "grid", axis=2, tiled=True),
        lax.all_gather(cotangent, "grid", axis=2, tiled=True),
        lax.all_gather(norm_gain[:, None, :], "grid", axis=2, tiled=True),
    )
    full_input = gathered[0][0]
    full_cot = gathered[1][0]
    full_gain = gathered[2][0, 0].astype(jnp.float32)
    weights = lax.all_gather(projections, "depth", axis=1, tiled=True)[0]
    tok_count = section_input.shape[1]
    width = weights.shape[0]
    inner = weights.shape[2]
    heads_here = head_gains.shape[2]
    head_dim = head_gains.shape[3]
    images = tok_count // SEQ
    score_scale = head_dim ** (-0.5)
    centred, reciprocal, centre = normalize(full_input.astype(jnp.float32))
    normed = (centred * full_gain).astype(jnp.bfloat16)
    projected = jnp.dot(
        normed, weights[:, :3].reshape(width, 3 * inner), preferred_element_type=jnp.float32
    )
    projected = projected.reshape(tok_count, 3, heads_here, head_dim)
    gains = head_gains[0].astype(jnp.float32)
    query_hat, query_rec, query_mid = normalize(projected[:, 0])
    key_hat, key_rec, key_mid = normalize(projected[:, 1])
    query_low = (query_hat * gains[0]).astype(jnp.bfloat16)
    key_low = (key_hat * gains[1]).astype(jnp.bfloat16)
    value_low = projected[:, 2].astype(jnp.bfloat16)

    def by_image(tensor):
        return tensor.reshape(images, SEQ, heads_here, head_dim)

    scores = (
        jnp.einsum(
            "ishd,ijhd->ihsj",
            by_image(query_low),
            by_image(key_low),
            preferred_element_type=jnp.float32,
        )
        * score_scale
    )
    exponent = jnp.exp(scores)
    attention = exponent / jnp.sum(exponent, axis=-1, keepdims=True)
    attention_low = attention.astype(jnp.bfloat16)
    attended = jnp.einsum(
        "ihsj,ijhd->ishd", attention_low, by_image(value_low), preferred_element_type=jnp.float32
    )
    attended = attended.astype(jnp.bfloat16).reshape(tok_count, inner)
    out_weight = weights[:, 3]
    out_partial = jnp.einsum("tk,dk->td", attended, out_weight, preferred_element_type=jnp.float32)
    branch = lax.psum_scatter(
        out_partial.astype(jnp.bfloat16), "grid", scatter_dimension=1, tiled=True
    )
    next_branch = shifted(branch[None], "section", 1)
    d_attended = jnp.dot(full_cot, out_weight, preferred_element_type=jnp.float32).astype(
        jnp.bfloat16
    )
    d_image = by_image(d_attended)
    d_attention = jnp.einsum(
        "ishd,ijhd->ihsj", d_image, by_image(value_low), preferred_element_type=jnp.float32
    )
    row_delta = jnp.sum(attention * d_attention, axis=-1, keepdims=True)
    d_score = (attention * (d_attention - row_delta) * score_scale).astype(jnp.bfloat16)
    d_query = jnp.einsum(
        "ihsj,ijhd->ishd", d_score, by_image(key_low), preferred_element_type=jnp.float32
    )
    d_query = d_query.reshape(tok_count, heads_here, head_dim)
    d_key = jnp.einsum(
        "ihsj,ishd->ijhd", d_score, by_image(query_low), preferred_element_type=jnp.float32
    )
    d_key = d_key.reshape(tok_count, heads_here, head_dim)
    d_value = jnp.einsum(
        "ihsj,ishd->ijhd", attention_low, d_image, preferred_element_type=jnp.float32
    )
    d_value = d_value.astype(jnp.bfloat16).reshape(tok_count, heads_here, head_dim)
    grad_query = normalize_back(d_query, query_hat, query_rec, gains[0]).astype(jnp.bfloat16)
    grad_key = normalize_back(d_key, key_hat, key_rec, gains[1]).astype(jnp.bfloat16)
    d_project = jnp.stack([grad_query, grad_key, d_value], axis=1).reshape(tok_count, 3, inner)
    grad_partial = jnp.einsum(
        "tck,dck->td", d_project, weights[:, :3], preferred_element_type=jnp.float32
    )
    d_normed = lax.psum_scatter(
        grad_partial.astype(jnp.bfloat16), "grid", scatter_dimension=1, tiled=True
    ).astype(jnp.float32)
    own_centred = (section_input[0].astype(jnp.float32) - centre) * reciprocal
    own_gain = norm_gain[0].astype(jnp.float32)
    weighted = d_normed * own_gain
    row_sums = lax.psum(
        (jnp.sum(weighted, axis=-1), jnp.sum(weighted * own_centred, axis=-1)), "grid"
    )
    first_mean = row_sums[0][:, None] / width
    second_mean = row_sums[1][:, None] / width
    input_grad = (reciprocal * (weighted - first_mean - own_centred * second_mean)).astype(
        jnp.bfloat16
    )
    returned_grad = shifted(input_grad[None], "section", -1)
    norm_part = jnp.sum(d_normed * own_centred, axis=0)
    head_part = jnp.stack([jnp.sum(d_query * query_hat, axis=0), jnp.sum(d_key * key_hat, axis=0)])
    norm_total, head_total = lax.psum((norm_part, head_part), "depth")
    moved_in, moved_cot = (
        lax.all_to_all(normed, "depth", split_axis=1, concat_axis=0, tiled=True),
        lax.all_to_all(full_cot, "depth", split_axis=1, concat_axis=0, tiled=True),
    )
    moved_project, moved_attended = (
        lax.all_gather(d_project, "depth", axis=0, tiled=True),
        lax.all_gather(attended, "depth", axis=0, tiled=True),
    )
    depth_count = lax.axis_size("depth")

    def by_group(tensor):
        return tensor.reshape((depth_count, tok_count) + tensor.shape[1:])

    part_qkv = jnp.einsum(
        "gtr,gtck->grck",
        by_group(moved_in),
        by_group(moved_project),
        preferred_element_type=jnp.float32,
    )
    part_out = jnp.einsum(
        "gtr,gtk->grk",
        by_group(moved_cot),
        by_group(moved_attended),
        preferred_element_type=jnp.float32,
    )
    stacked = (
        jnp.concatenate([part_qkv, part_out[:, :, None]], axis=2)
        .astype(jnp.bfloat16)
        .astype(jnp.float32)
    )
    weight_grad = jnp.sum(stacked, axis=0).astype(jnp.bfloat16)
    return (next_branch, returned_grad, weight_grad[None], norm_total[None], head_total[None])


def solution(mesh):
    in_specs = (
        P("section", "depth", "grid"),
        P("section", "depth", "grid"),
        P("section", "depth", None, "grid"),
        P("section", "grid"),
        P("section", None, "grid", None),
    )
    out_specs = (
        P("section", "depth", "grid"),
        P("section", "depth", "grid"),
        P("section", "depth", None, "grid"),
        P("section", "grid"),
        P("section", None, "grid", None),
    )
    return jax.shard_map(local, mesh=mesh, in_specs=in_specs, out_specs=out_specs, check_vma=False)
```

profile of v0, /device:TPU:32, one launch (start us, length us, event | category | flops | bytes accessed | tf_op | source)
XLA Modules:
  0.0 673.1 jit_solution(12691836196823777841)
XLA Ops:
  7.9 4.0 copy.45
  13.7 18.3 %all-gather = bf16[1,6144]{1,0:T(2,128)(2,1)S(1)} all-gather(bf16[1,384]{1,0:T(2,128)(2,1)S(1)} %copy-done.11), channel_id=2, replica_groups=mesh['section'=4,'depth'=4,'grid'=16] {'grid'}, dimensions={1}, use_global_device_ids=true | all-gather | bytes 13056 | tf_op jit(solution)/shard_map/all_gather | solution.py:35
  32.7 18.1 %all-gather.6.cloned.1.call-done = bf16[1,256,6144]{2,1,0:T(8,128)(2,1)} async-done(((bf16[1,256,384]{2,1,0:T(8,128)(2,1)}), bf16[1,256,6144]{2,1,0:T(8,128)(2,1)}) %all-gather.6.cloned.1.call-update) | async-done | bytes 3145744 | tf_op jit(solution)/shard_map/all_gather | solution.py:33
  54.0 223.8 %all-gather.8.cloned.1.call-done = bf16[1,6144,4,256]{3,1,2,0:T(8,128)(2,1)} async-done(((bf16[1,1536,4,256]{3,1,2,0:T(8,128)(2,1)}), bf16[1,6144,4,256]{3,1,2,0:T(8,128)(2,1)}) %all-gather.8.cloned.1.call-update) | async-done | bytes 12582928 | tf_op jit(solution)/shard_map/all_gather | solution.py:40
  277.8 7.9 %slice.34 = bf16[6144,3,256]{2,0,1:T(8,128)(2,1)} slice(bf16[6144,4,256]{2,0,1:T(8,128)(2,1)} %bitcast.173), slice={[0:6144], [0:3], [0:256]} | slice | bytes 18874368 | tf_op jit(solution)/shard_map/slice | solution.py:51
  285.7 12.5 %copy.46 = bf16[6144,3,256]{0,2,1:T(8,128)(2,1)} copy(bf16[6144,3,256]{2,0,1:T(8,128)(2,1)} %slice.34) | data formatting | bytes 18874368 | tf_op jit(solution)/shard_map/slice | solution.py:51
  298.2 5.6 fusion.4
  305.4 11.8 %all-gather.10.cloned.1.call-done = bf16[1,256,6144]{1,2,0:T(8,128)(2,1)} async-done(((bf16[1,256,384]{1,2,0:T(8,128)(2,1)}), bf16[1,256,6144]{1,2,0:T(8,128)(2,1)}) %all-gather.10.cloned.1.call-update) | async-done | bytes 3145744 | tf_op jit(solution)/shard_map/all_gather | solution.py:34
  317.2 4.2 fusion.19
  335.3 6.2 all-to-all-start.1
  344.3 5.4 copy.59
  349.8 8.1 %fusion.1 = bf16[256,6144]{1,0:T(8,128)(2,1)} fusion(bf16[256,1,256]{2,0,1:T(8,128)(2,1)S(1)} %copy.58, bf16[256,1,256]{2,0,1:T(8,128)(2,1)S(1)} %copy.57, bf16[256,1,256]{2,0,1:T(8,128)(2,1)} %copy-done.6, bf16[6144,4,256]{2,0,1:T(8,128)(2,1)} %bitcast.176), kind=kOutput, calls=%fused_computation.4 | convolution fusion | flops 2417885184 | bytes 12976128 | tf_op jit(solution)/shard_map/tck,dck->td/dot_general | solution.py:110
  357.8 4.7 copy.80
  363.2 4.5 multiply_convert_fusion
  367.7 71.0 %all-to-all-done.1 = bf16[256,4,1536]{2,0,1:T(8,128)(2,1)S(1)} async-done(((bf16[256,4,1536]{2,0,1:T(8,128)(2,1)}), bf16[256,4,1536]{2,0,1:T(8,128)(2,1)S(1)}, u32[]{:S(2)}, u32[]{:S(2)}) %all-to-all-start.1) | async-done | bytes 3145760 | tf_op jit(solution)/shard_map/all_to_all | solution.py:133
  440.5 3.7 all-to-all-start
  444.9 92.2 %all_gather.23 = bf16[1024,256]{1,0:T(8,128)(2,1)S(1)} all-gather(bf16[256,256]{1,0:T(8,128)(2,1)S(1)} %copy.61), channel_id=1, replica_groups=mesh['section'=4,'depth'=4,'grid'=16] {'depth'}, dimensions={0}, use_global_device_ids=true | all-gather | bytes 655360 | tf_op jit(solution)/shard_map/all_gather | solution.py:137
  537.2 4.9 fusion.2
  542.0 6.5 convolution_convert_fusion.1
  550.3 45.9 %reduce-scatter.9.cloned.1.call-done = bf16[384,256]{1,0:T(8,128)(2,1)} async-done(((bf16[6144,256]{1,0:T(8,128)(2,1)}), bf16[384,256]{1,0:T(8,128)(2,1)}) %reduce-scatter.9.cloned.1.call-update) | async-done | bytes 196624
  597.5 28.6 %all-reduce = (f32[256]{0:T(256)S(1)}, f32[256]{0:T(256)S(1)}) all-reduce(f32[256]{0:T(256)S(1)} %get-tuple-element.23, f32[256]{0:T(256)S(1)} %get-tuple-element.26), channel_id=1, replica_groups=mesh['section'=4,'depth'=4,'grid'=16] {'grid'}, use_global_device_ids=true, to_apply=%region_17.0 | all-reduce | flops 512 | bytes 4096 | tf_op jit(solution)/shard_map/psum | solution.py:119
  629.8 9.5 %maximum_reduce_fusion = bf16[1536,4,256]{2,0,1:T(8,128)(2,1)S(1)} fusion(bf16[4,1536,1,256]{3,1,2,0:T(8,128)(2,1)} %fusion.2, bf16[4,1536,3,256]{3,1,2,0:T(8,128)(2,1)} %convolution_convert_fusion.1), kind=kLoop, calls=%fused_computation.1 | loop fusion | flops 11010048 | bytes 15728640 | tf_op jit(solution)/shard_map/reduce_sum | solution.py:161
  639.3 13.1 %copy.65 = bf16[1,1536,4,256]{3,2,1,0:T(4,128)(2,1)} copy(bf16[1,1536,4,256]{3,1,2,0:T(8,128)(2,1)S(1)} %bitcast.179) | data formatting | bytes 6291456
  652.4 12.4 %all-reduce.1 = (f32[1,384]{1,0:T(1,128)}, f32[1,2,2,128]{3,2,1,0:T(2,128)}) all-reduce(f32[1,384]{1,0:T(1,128)S(1)} %broadcast_in_dim.20, f32[1,2,2,128]{3,2,1,0:T(2,128)S(1)} %copy-done.10), channel_id=1, replica_groups=mesh['section'=4,'depth'=4,'grid'=16] {'depth'}, use_global_device_ids=true, to_apply=%region_20.0 | all-reduce | flops 896 | bytes 7168 | tf_op jit(solution)/shard_map/psum | solution.py:130
  (92 shorter events, 35.9 us)
Async XLA Ops:
  7.2 43.6 %all-gather.6.cloned.1.call-start = ((), (), s32[]{:S(2)}) async-start(), calls=%async_computation.4 | async-start | bytes 3342336 | tf_op jit(solution)/shard_map/all_gather | solution.py:33
  7.9 269.9 %all-gather.8.cloned.1.call-start = ((), (), s32[]{:S(2)}) async-start(), calls=%async_computation.5 | async-start | bytes 15728640 | tf_op jit(solution)/shard_map/all_gather | solution.py:40
  11.9 0.9 copy-start.8
  11.9 1.8 copy-start.11
  11.9 20.7 %copy-start.12 = (bf16[1,2,2,128]{3,2,1,0:T(2,128)(2,1)S(1)}, bf16[1,2,2,128]{3,2,1,0:T(2,128)(2,1)}, u32[]{:S(2)}) copy-start(bf16[1,2,2,128]{3,2,1,0:T(2,128)(2,1)} %param.9) | copy-start | bytes 3076
  11.9 305.3 %all-gather.10.cloned.1.call-start = ((), (), s32[]{:S(2)}) async-start(), calls=%async_computation.6 | async-start | bytes 3342336 | tf_op jit(solution)/shard_map/all_gather | solution.py:34
  13.7 528.4 %all-gather.12.cloned.1.call-start = ((), (), s32[]{:S(2)}) async-start(), calls=%async_computation.7 | async-start | bytes 1966080 | tf_op jit(solution)/shard_map/all_gather | solution.py:136
  285.7 12.5 %copy-start.1 = (bf16[1,256,6144]{2,1,0:T(8,128)(2,1)S(1)}, bf16[1,256,6144]{2,1,0:T(8,128)(2,1)}, u32[]{:S(2)}) copy-start(bf16[1,256,6144]{2,1,0:T(8,128)(2,1)} %all-gather.6.cloned.1.call-done) | copy-start | bytes 9437188
  303.7 0.9 copy-start.2
  305.4 16.0 %copy-start.3 = (f32[256,3,2,128]{0,3,2,1:T(8,128)S(1)}, f32[256,3,2,128]{0,3,2,1:T(8,128)}, u32[]{:S(2)}) copy-start(f32[256,3,2,128]{0,3,2,1:T(8,128)} %copy-done.2) | copy-start | bytes 2359300
  323.8 1.2 copy-start.6
  324.6 223.9 %reduce-scatter.7.cloned.1.call-start = ((), (), s32[]{:S(2)}) async-start(), calls=%async_computation.8 | async-start | bytes 3342336
  330.6 1.9 copy-start.4
  335.3 103.4 %all-to-all-start.1 = ((bf16[256,4,1536]{2,0,1:T(8,128)(2,1)}), bf16[256,4,1536]{2,0,1:T(8,128)(2,1)S(1)}, u32[]{:S(2)}, u32[]{:S(2)}) async-start(bf16[256,4,1536]{2,0,1:T(8,128)(2,1)} %copy.62), calls=%async_computation.1 | async-start | bytes 6291456 | tf_op jit(solution)/shard_map/all_to_all | solution.py:133
  341.6 254.6 %reduce-scatter.9.cloned.1.call-start = ((), (), s32[]{:S(2)}) async-start(), calls=%async_computation.9 | async-start | bytes 3342336
  362.5 0.7 copy-start.9
  367.7 76.6 %copy-start.13 = (f32[2,128]{1,0:T(2,128)S(1)}, f32[2,128]{1,0:T(2,128)}, u32[]{:S(2)}) copy-start(f32[2,128]{1,0:T(2,128)} %get-tuple-element.12) | copy-start | bytes 3076
  367.7 76.6 %copy-start.14 = (f32[2,128]{1,0:T(2,128)S(1)}, f32[2,128]{1,0:T(2,128)}, u32[]{:S(2)}) copy-start(f32[2,128]{1,0:T(2,128)} %get-tuple-element.17) | copy-start | bytes 3076
  438.8 1.7 copy-start
  440.5 101.6 %all-to-all-start = ((bf16[256,4,1536]{0,2,1:T(8,128)(2,1)}), bf16[256,4,1536]{0,2,1:T(8,128)(2,1)S(1)}, u32[]{:S(2)}, u32[]{:S(2)}) async-start(bf16[256,4,1536]{0,2,1:T(8,128)(2,1)} %multiply_convert_fusion), calls=%async_computation | async-start | bytes 6291456 | tf_op jit(solution)/shard_map/all_to_all | solution.py:132
  542.0 55.2 %copy-start.5 = (bf16[1,256,384]{2,1,0:T(8,128)(2,1)S(1)}, bf16[1,256,384]{2,1,0:T(8,128)(2,1)}, u32[]{:S(2)}) copy-start(bf16[1,256,384]{2,1,0:T(8,128)(2,1)} %param.5) | copy-start | bytes 589828
  550.3 114.6 %collective-permute-start = (bf16[1,256,384]{2,1,0:T(8,128)(2,1)}, bf16[1,256,384]{2,1,0:T(8,128)(2,1)S(1)}, u32[]{:S(2)}, u32[]{:S(2)}) collective-permute-start(bf16[1,256,384]{2,1,0:T(8,128)(2,1)} %bitcast.17), channel_id=1, source_target_pairs={{0,64},{64,128},{128,192},{192,0},{1,65},{65,129},{129,193},{193,1... | collective-permute-start | bytes 589832 | tf_op jit(solution)/shard_map/ppermute | solution.py:14
  627.0 37.8 %collective-permute-start.1 = (bf16[1,256,384]{2,1,0:T(8,128)(2,1)}, bf16[1,256,384]{2,1,0:T(8,128)(2,1)S(1)}, u32[]{:S(2)}, u32[]{:S(2)}) collective-permute-start(bf16[1,256,384]{2,1,0:T(8,128)(2,1)} %fusion.58), channel_id=1, source_target_pairs={{0,192},{64,0},{128,64},{192,128},{1,193},{65,1},{129,65},{193,129... | collective-permute-start | bytes 589832 | tf_op jit(solution)/shard_map/ppermute | solution.py:14
  639.3 13.1 %copy-start.10 = (f32[1,2,2,128]{3,2,1,0:T(2,128)S(1)}, f32[1,2,2,128]{3,2,1,0:T(2,128)}, u32[]{:S(2)}) copy-start(f32[1,2,2,128]{3,2,1,0:T(2,128)} %maximum_bitcast_fusion) | copy-start | bytes 6148
  (1 other events, 0.6 us)
Sparse Core Ops, SparseCore 0:
  9.8 40.9 all-gather.5
  53.2 224.6 all-gather.7
  280.2 36.9 all-gather.9
  324.7 76.2 all-gather.11
  404.0 108.4 reduce-scatter.6
  514.9 81.2 reduce-scatter.8
where the time goes:
time: 674 us; the launch traced here: 673 us
  waiting for transfers between devices  371 us (55%)
  blocking collectives  152 us (23%)
  local copies, waits for them, and re-layouts  66.3 us (10%)
  matrix products  34.8 us (5%)
  other arithmetic  21.7 us (3%)
  between operations  14.4 us (2%)
  starting transfers between devices  12.9 us (2%)
    all_gather x1, waiting for transfers between devices, local(): weights = lax.all_gather(projections, 'depth', axis=1, tiled=True)[0]  224 us
    all_gather x1, blocking collectives, local(): lax.all_gather(attended, 'depth', axis=0, tiled=True)  92.2 us
    all_to_all x1, waiting for transfers between devices, local(): lax.all_to_all(full_cot, 'depth', split_axis=1, concat_axis=0, tiled=True)  71 us
    unnamed x8, waiting for transfers between devices  46.6 us
    unnamed x39, local copies, waits for them, and re-layouts  36 us
    psum x1, blocking collectives, local(): lax.psum((jnp.sum(weighted, axis=-1), jnp.sum(weighted * own_centred, axi...  28.6 us
    slice x2, local copies, waits for them, and re-layouts, local(): weights[:, :3].reshape(width, 3 * inner)  20.3 us
    all_gather x1, blocking collectives, local(): lax.all_gather(norm_gain[:, None, :], 'grid', axis=2, tiled=True)  18.3 us
  transfers between devices with their start and end apart: 10, of which 5 were waited for; matrix products, arithmetic and copies ran while one was open for 16% of the time, Pallas kernels for 0%

commit v1 on v0

v1 whole, which is shorter than its diff:
```python
from types import SimpleNamespace

import jax
import jax.numpy as jnp
from jax import lax
from jax.experimental import pallas as pl
from jax.experimental.pallas import tpu as pltpu
from jax.sharding import PartitionSpec as P

SEQ = 256
HALF = 128
QUARTER = 64
EPSILON = 1e-06
MESH = pl.DeviceIdType.MESH
BF16 = jnp.bfloat16
F32 = jnp.float32
FEATURES = 384
ROWS = 1536
HEAD = 128
QKV = 768
COLS = 1024
GRID = 16
SCALE = HEAD ** (-0.5)


def remote(src, dst, send_sem, recv_sem, device):
    return pltpu.make_async_remote_copy(
        src_ref=src,
        dst_ref=dst,
        send_sem=send_sem,
        recv_sem=recv_sem,
        device_id=device,
        device_id_type=MESH,
    )


def normalize(values):
    centre = jnp.mean(values, axis=-1, keepdims=True)
    second = jnp.mean(values * values, axis=-1, keepdims=True)
    reciprocal = lax.rsqrt(second - centre * centre + EPSILON)
    return (values - centre) * reciprocal, reciprocal


def normalize_back(upstream, normed, reciprocal, gain_row):
    scaled = upstream * gain_row
    first_mean = jnp.mean(scaled, axis=-1, keepdims=True)
    second_mean = jnp.mean(scaled * normed, axis=-1, keepdims=True)
    return reciprocal * (scaled - first_mean - normed * second_mean)


def dot(a, b):
    return jnp.dot(a, b, preferred_element_type=F32)


def dot_nt(a, b):
    return lax.dot_general(a, b, (((1,), (1,)), ((), ())), preferred_element_type=F32)


def dot_tn(a, b):
    return lax.dot_general(a, b, (((0,), (0,)), ((), ())), preferred_element_type=F32)


def vmem(shape, dtype):
    return pltpu.VMEM(shape, dtype)


def dma(count):
    return pltpu.SemaphoreType.DMA((count,))


def gather_scratch():
    return dict(
        own_send=dma(4),
        near_recv=dma(4),
        side_send=dma(8),
        side_recv=dma(8),
        far_send=dma(8),
        far_recv=dma(8),
        sib_send=dma(16),
        sib_recv=dma(16),
        half_send=dma(2),
        half_recv=dma(2),
        full_send=dma(4),
        full_recv=dma(4),
        ring_send=dma(6),
        ring_recv=dma(6),
    )


def reduce_scratch():
    return dict(
        sib_out=vmem((8, SEQ, FEATURES), BF16),
        sib_in=vmem((8, SEQ, FEATURES), BF16),
        keep=vmem((8, SEQ, FEATURES), F32),
        far_out=vmem((8, QUARTER, FEATURES), BF16),
        far_in=vmem((8, QUARTER, FEATURES), BF16),
        side_out=vmem((8, HALF, FEATURES), BF16),
        side_in=vmem((8, HALF, FEATURES), BF16),
        total=vmem((4, HALF, FEATURES), F32),
        next_out=vmem((4, HALF, FEATURES), BF16),
        mate_in=vmem((4, HALF, FEATURES), BF16),
        last_in=vmem((4, HALF, FEATURES), BF16),
        r_sib_send=dma(8),
        r_sib_recv=dma(8),
        r_far_send=dma(8),
        r_far_recv=dma(8),
        r_side_send=dma(8),
        r_side_recv=dma(8),
        r_next_send=dma(4),
        r_mate_recv=dma(4),
        r_last_recv=dma(4),
    )


def sum_scratch(count, rows, columns):
    return dict(
        out=vmem((rows, columns), F32),
        slots=vmem((count, rows, columns), F32),
        send=dma(count),
        recv=dma(count),
    )


SCRATCH = dict(
    acts=gather_scratch(),
    cots=gather_scratch(),
    branch=reduce_scratch(),
    inputs=reduce_scratch(),
    stat_a=sum_scratch(GRID, 8, SEQ),
    stat_b=sum_scratch(GRID, 8, SEQ),
    gains=sum_scratch(4, 8, HEAD),
    norms=sum_scratch(4, 8, FEATURES),
    sems=dict(w=dma(1), grad_send=dma(1), grad_recv=dma(1)),
    buf=dict(
        w=vmem((ROWS, COLS), BF16),
        norm=vmem((SEQ, FEATURES), BF16),
        centred=vmem((SEQ, FEATURES), F32),
        recip=vmem((SEQ, HEAD), F32),
        big_x=vmem((4 * SEQ, ROWS), BF16),
        big_c=vmem((4 * SEQ, ROWS), BF16),
        far_out=vmem((SEQ, COLS), BF16),
        up_out=vmem((SEQ, COLS), BF16),
        down_out=vmem((SEQ, COLS), BF16),
        half_minus=vmem((SEQ, COLS), BF16),
        half_plus=vmem((SEQ, COLS), BF16),
        full_minus=vmem((SEQ, COLS), BF16),
        full_plus=vmem((SEQ, COLS), BF16),
        up_acc=vmem((SEQ, COLS), F32),
        down_acc=vmem((SEQ, COLS), F32),
        own_acc=vmem((SEQ, COLS), F32),
        attention=vmem((2, SEQ, SEQ), F32),
        hats=vmem((4, SEQ, HEAD), F32),
        recs=vmem((4, SEQ, HEAD), F32),
        lows=vmem((6, SEQ, HEAD), BF16),
        att=vmem((4 * SEQ, 256), BF16),
        dp=vmem((4 * SEQ, QKV), BF16),
        grad_out=vmem((SEQ, FEATURES), BF16),
        grad_in=vmem((SEQ, FEATURES), BF16),
    ),
)
LEAVES, TREE = jax.tree.flatten(SCRATCH)


def kernel(*refs):
    x_ref, cot_ref, w_hbm, ng_ref, hg_ref = refs[:5]
    nb_ref, rg_ref, dw_ref, ngg_ref, hgg_ref = refs[5:10]
    parts = jax.tree.unflatten(TREE, refs[10:])
    parts = {name: SimpleNamespace(**part) for name, part in parts.items()}
    acts, cots, branch, inputs = (parts[name] for name in ("acts", "cots", "branch", "inputs"))
    stat_a, stat_b, gains, norms = (parts[name] for name in ("stat_a", "stat_b", "gains", "norms"))
    sems, buf = parts["sems"], parts["buf"]
    w = buf.w

    s = lax.axis_index("section")
    d = lax.axis_index("depth")
    g = lax.axis_index("grid")
    z = g // 8
    x = (g // 2) % 4
    c = g % 2
    base = 2 * (d % 2)
    place = (x - base + 4) % 4
    up = (d + 1) % 4
    down = (d + 3) % 4
    across = (d + 2) % 4

    def at(depth, z_, x_, c_, section=None):
        return (s if section is None else section, depth, z_ * 8 + x_ * 2 + c_)

    sibling = at(d, z, x, 1 - c)
    left_x = (x + 3) % 4
    right_x = (x + 1) % 4
    places = (x, left_x, right_x, (x + 2) % 4)
    left = at(d, z, left_x, c)
    right = at(d, z, right_x, c)
    above = at(up, z, x, c)
    below = at(down, z, x, c)
    section_up = (s + 1) % 4
    section_down = (s + 3) % 4
    home = g // 4
    home_block = g % 4
    home_base = 2 * (home % 2)
    home_other = (home_base + 3 - (x - home_base + 4) % 4) % 4
    owner_x = base + ((place + 1) // 2) % 2
    mate = at(d, 1 - z, x, c)

    def entry(t, depth):
        k = (t - depth + 4) % 4
        middle = depth // 2
        return (k % 2) * ((3 - k) // 2) + (1 - k % 2) * (middle + (k // 2) * (1 - 2 * middle))


    barrier = pltpu.get_barrier_semaphore()

    def greet(device):
        pl.semaphore_signal(barrier, inc=1, device_id=device, device_id_type=MESH)

    for k in range(1, GRID):
        greet((s, d, (g + k) % GRID))
    for k in range(1, 4):
        greet(at((d + k) % 4, z, x, c))
        greet(at((d + k) % 4, d // 2, owner_x, c))
    greet((section_up, d, g))
    for zz in range(2):
        for xx in (x, home_other):
            greet(at(home, zz, xx, c, section_down))

    @pl.when(home != d)
    def _():
        for zz in range(2):
            for xx in (x, home_other):
                greet(at(home, zz, xx, c))

    pl.semaphore_wait(barrier, 26 + 4 * (((home - d + 4) % 4 + 3) // 4))

    w_copy = pltpu.make_async_copy(w_hbm, w, sems.w.at[0])
    w_copy.start()

    def tokens(t):
        return pl.ds(pl.multiple_of(t * SEQ, SEQ), SEQ)

    def features(j):
        return pl.ds(pl.multiple_of(j * FEATURES, FEATURES), FEATURES)

    def own_copy(src, big, kind, h, zz):
        rows = pl.ds(pl.multiple_of(d * SEQ + h * HALF, HALF), HALF)
        return remote(
            src.at[h * HALF : (h + 1) * HALF, :],
            big.at[rows, features(home_block)],
            kind.own_send.at[2 * h + zz],
            kind.near_recv.at[d],
            at(home, zz, home_other if h else x, c),
        )

    def own_send(src, big, kind):
        for zz in range(2):
            here = jnp.logical_and(home == d, z == zz)

            @pl.when(here)
            def _():
                pltpu.make_async_copy(
                    src.at[0:HALF, :],
                    big.at[pl.ds(pl.multiple_of(d * SEQ, SEQ), HALF), features(home_block)],
                    kind.near_recv.at[d],
                ).start()

            @pl.when(jnp.logical_not(here))
            def _():
                own_copy(src, big, kind, 0, zz).start()

            own_copy(src, big, kind, 1, zz).start()

    def block(big, t, x_, c_, lo=0, count=HALF):
        p = (x_ - base + 4) % 4
        start = pl.multiple_of(t * SEQ + (p // 2) * HALF + lo, QUARTER)
        return big.at[pl.ds(start, count), features(2 * (((p + 1) // 2) % 2) + c_)]

    def side_copy(big, kind, t, side, arriving=False):
        ref = block(big, t, places[1 + side] if arriving else x, c)
        slot = 2 * t + side
        return remote(
            ref, ref, kind.side_send.at[slot], kind.side_recv.at[slot], (right, left)[side]
        )

    def far_copy(big, kind, t, side, arriving=False):
        ref = block(big, t, places[3 if arriving else 1 + side], c, side * QUARTER, QUARTER)
        slot = 2 * t + side
        return remote(
            ref, ref, kind.far_send.at[slot], kind.far_recv.at[slot], (right, left)[side]
        )

    def sib_copy(big, kind, t, part, arriving=False):
        ref = block(big, t, places[part], 1 - c if arriving else c)
        slot = 4 * t + part
        return remote(ref, ref, kind.sib_send.at[slot], kind.sib_recv.at[slot], sibling)

    def near_step(big, kind, t):
        ref = block(big, t, x, c)
        remote(ref, ref, kind.side_send.at[2 * t], kind.near_recv.at[t], right).wait_recv()
        side_copy(big, kind, t, 0).start()
        side_copy(big, kind, t, 1).start()
        sib_copy(big, kind, t, 0).start()

    def side_sent(big, kind, t):
        side_copy(big, kind, t, 0).wait_send()
        side_copy(big, kind, t, 1).wait_send()

    def side_step(big, kind, t):
        for side in range(2):
            side_copy(big, kind, t, side, True).wait_recv()
            far_copy(big, kind, t, side).start()
            sib_copy(big, kind, t, 1 + side).start()

    def far_step(big, kind, t):
        far_copy(big, kind, t, 0, True).wait_recv()
        far_copy(big, kind, t, 1, True).wait_recv()
        sib_copy(big, kind, t, 3).start()

    def sib_step(big, kind, t):
        for part in range(4):
            sib_copy(big, kind, t, part, True).wait_recv()

    def drain_gather(src, big, kind):
        for zz in range(2):

            @pl.when(jnp.logical_or(home != d, z != zz))
            def _():
                own_copy(src, big, kind, 0, zz).wait_send()

            own_copy(src, big, kind, 1, zz).wait_send()
        for t in range(4):
            for part in range(4):
                sib_copy(big, kind, t, part).wait_send()
            far_copy(big, kind, t, 0).wait_send()
            far_copy(big, kind, t, 1).wait_send()

    def half_copy(kind, lo, count, side):
        cut = lo + side * (count // 2)
        cols = slice(cut, cut + count // 2)
        dst = buf.half_minus if side == 0 else buf.half_plus
        return remote(
            buf.far_out.at[:, cols],
            dst.at[:, cols],
            kind.half_send.at[side],
            kind.half_recv.at[side],
            above if side == 0 else below,
        )

    def full_copy(kind, lo, count, side, part):
        cut = lo + part * (count // 2)
        cols = slice(cut, cut + count // 2)
        src = buf.up_out if side == 0 else buf.down_out
        dst = buf.full_minus if side == 0 else buf.full_plus
        return remote(
            src.at[:, cols],
            dst.at[:, cols],
            kind.full_send.at[2 * side + part],
            kind.full_recv.at[2 * side + part],
            above if side == 0 else below,
        )

    def pass_on(kind, lo, count, side, part):
        acc = buf.up_acc if side == 0 else buf.down_acc
        out = buf.up_out if side == 0 else buf.down_out
        got = buf.half_minus if side == 0 else buf.half_plus
        cut = lo + part * (count // 2)
        cols = slice(cut, cut + count // 2)
        value = acc[:, cols]
        if part == side:
            half_copy(kind, lo, count, side).wait_recv()
            value = value + got[:, cols].astype(F32)
        out[:, cols] = value.astype(BF16)
        full_copy(kind, lo, count, side, part).start()

    def multiply(big, kind, lo, count, t, ref):
        sib_step(big, kind, t)
        for q in range(lo, lo + count, 256):
            ref[:, q : q + 256] = dot(big[tokens(t), :], w[:, q : q + 256]).astype(ref.dtype)

    def multiply_step(big, kind, lo, count, r):
        if r == 0:
            multiply(big, kind, lo, count, d, buf.own_acc)
        elif r == 1:
            multiply(big, kind, lo, count, up, buf.up_acc)
            pass_on(kind, lo, count, 0, 1)
        elif r == 3:
            multiply(big, kind, lo, count, down, buf.down_acc)
            pass_on(kind, lo, count, 1, 0)
        else:
            multiply(big, kind, lo, count, across, buf.far_out)
            half_copy(kind, lo, count, 0).start()
            half_copy(kind, lo, count, 1).start()

    def finish_depth(kind, lo, count):
        cols = slice(lo, lo + count)
        for side in range(2):
            full_copy(kind, lo, count, side, 0).wait_recv()
            full_copy(kind, lo, count, side, 1).wait_recv()
        buf.own_acc[:, cols] = (
            buf.own_acc[:, cols]
            + buf.full_minus[:, cols].astype(F32)
            + buf.full_plus[:, cols].astype(F32)
        )

    def drain_depth(kind, lo, count):
        for side in range(2):
            half_copy(kind, lo, count, side).wait_send()
            full_copy(kind, lo, count, side, 0).wait_send()
            full_copy(kind, lo, count, side, 1).wait_send()

    def ring_block(ref, step, t):
        half = ref.shape[1] // 2
        second = step in (1, 2, 5)
        return ref.at[tokens(t), half:] if second else ref.at[tokens(t), :half]

    def ring_copy(ref, kind, step):
        block = ring_block(ref, step, (d, d, d, d, down, up)[step])
        return remote(
            block,
            block,
            kind.ring_send.at[step],
            kind.ring_recv.at[step],
            above if step % 2 == 0 else below,
        )

    def ring_wait(ref, kind, step):
        block = ring_block(ref, step, (down, up, down, up, across, across)[step])
        remote(
            block,
            block,
            kind.ring_send.at[step],
            kind.ring_recv.at[step],
            above if step % 2 == 0 else below,
        ).wait_recv()

    def ring_start(ref, kind):
        ring_copy(ref, kind, 0).start()
        ring_copy(ref, kind, 1).start()

    def ring_more(ref, kind):
        for step in range(2):
            ring_copy(ref, kind, step).wait_send()
            ring_copy(ref, kind, step + 2).start()

    def ring_forward(ref, kind):
        for step in range(2):
            ring_wait(ref, kind, step)
            ring_copy(ref, kind, step + 2).wait_send()
            ring_copy(ref, kind, step + 4).start()

    def ring_near(ref, kind):
        ring_wait(ref, kind, 2)
        ring_wait(ref, kind, 3)

    def ring_far(ref, kind):
        ring_wait(ref, kind, 4)
        ring_wait(ref, kind, 5)

    def r_sib(kind, t, i):
        slot = 2 * t + i
        return remote(
            kind.sib_out.at[slot],
            kind.sib_in.at[slot],
            kind.r_sib_send.at[slot],
            kind.r_sib_recv.at[slot],
            sibling,
        )

    def r_far(kind, t, side):
        slot = 2 * t + side
        return remote(
            kind.far_out.at[slot],
            kind.far_in.at[slot],
            kind.r_far_send.at[slot],
            kind.r_far_recv.at[slot],
            (right, left)[side],
        )

    def r_side(kind, t, side):
        slot = 2 * t + side
        return remote(
            kind.side_out.at[slot],
            kind.side_in.at[slot],
            kind.r_side_send.at[slot],
            kind.r_side_recv.at[slot],
            (right, left)[side],
        )

    def r_mate(kind, t):
        return remote(
            kind.next_out.at[t],
            kind.mate_in.at[t],
            kind.r_next_send.at[t],
            kind.r_mate_recv.at[t],
            mate,
        )

    def r_last(kind, t, act):
        slot = place // 2 if kind is branch else 2 * (place // 2) + z
        dst = kind.last_in.at[slot]
        recv = kind.r_last_recv.at[slot]
        src = kind.next_out.at[t]
        section = section_up if kind is branch else s
        copy = remote(src, dst, kind.r_next_send.at[t], recv, at(t, d // 2, owner_x, c, section))

        def away():
            if act == "start":
                copy.start()
            else:
                copy.wait_send()

        if kind is branch:
            away()
        else:
            here = jnp.logical_and(t == d, jnp.logical_and(place < 2, z == d // 2))
            pl.when(jnp.logical_not(here))(away)

            @pl.when(here)
            def _():
                if act == "start":
                    pltpu.make_async_copy(src, dst, recv).start()

    def total_of(kind, t, x_, lo, count):
        p = (x_ - base + 4) % 4
        slot = 2 * t + ((p + 1) // 2) % 2
        rows = pl.ds(pl.multiple_of((p // 2) * HALF + lo, QUARTER), count)
        return kind.keep[slot, rows, :] + kind.sib_in[slot, rows, :].astype(F32)

    def first_stage(ref, kind, lo, t):
        count = ref.shape[1]
        left = ref[tokens(t), :]
        for i in range(2):
            rows = features(2 * i + 1 - c)
            value = dot_nt(left, w[rows, lo : lo + count])
            kind.sib_out[2 * t + i] = value.astype(BF16)
            r_sib(kind, t, i).start()
        for i in range(2):
            rows = features(2 * i + c)
            kind.keep[2 * t + i] = dot_nt(left, w[rows, lo : lo + count])

    def second_stage(kind, t):
        r_sib(kind, t, 0).wait_recv()
        r_sib(kind, t, 1).wait_recv()
        for side in range(2):
            value = total_of(kind, t, places[3], side * QUARTER, QUARTER)
            kind.far_out[2 * t + side] = value.astype(BF16)
            r_far(kind, t, side).start()

    def third_stage(kind, t):
        for side in range(2):
            slot = 2 * t + side
            r_far(kind, t, side).wait_recv()
            for part in range(2):
                value = total_of(kind, t, places[2 - side], part * QUARTER, QUARTER)
                if part == side:
                    value = value + kind.far_in[slot].astype(F32)
                kind.side_out[slot, part * QUARTER : (part + 1) * QUARTER, :] = value.astype(BF16)
            r_side(kind, t, side).start()

    def side_done(kind, t):
        r_side(kind, t, 0).wait_send()
        r_side(kind, t, 1).wait_send()

    def fourth_stage(kind, t):
        r_side(kind, t, 0).wait_recv()
        r_side(kind, t, 1).wait_recv()
        total = total_of(kind, t, x, 0, HALF)
        total = total + kind.side_in[2 * t].astype(F32) + kind.side_in[2 * t + 1].astype(F32)
        if kind is inputs:
            kind.next_out[t] = total.astype(BF16)
            r_last(kind, t, "start")
            return
        kind.total[t] = total

        @pl.when(z != entry(t, d))
        def _():
            kind.next_out[t] = total.astype(BF16)
            r_mate(kind, t).start()

    def fifth_stage(kind, t):
        @pl.when(z == entry(t, d))
        def _():
            r_mate(kind, t).wait_recv()
            total = kind.total[t] + kind.mate_in[t].astype(F32)
            kind.next_out[t] = total.astype(BF16)
            r_last(kind, t, "start")

    def last_stage(kind):
        count = 2 if kind is branch else 4
        for slot in range(count):
            remote(
                kind.last_in.at[slot],
                kind.last_in.at[slot],
                kind.r_next_send.at[0],
                kind.r_last_recv.at[slot],
                sibling,
            ).wait_recv()
        if kind is branch:
            return kind.last_in[0:2].reshape(SEQ, FEATURES).astype(F32)
        halves = [
            kind.last_in[2 * h].astype(F32) + kind.last_in[2 * h + 1].astype(F32) for h in range(2)
        ]
        return jnp.concatenate(halves, axis=0)

    def drain_reduce(kind):
        for t in range(4):
            r_sib(kind, t, 0).wait_send()
            r_sib(kind, t, 1).wait_send()
            r_far(kind, t, 0).wait_send()
            r_far(kind, t, 1).wait_send()

            if kind is inputs:
                r_last(kind, t, "wait")
                continue

            @pl.when(z != entry(t, d))
            def _():
                r_mate(kind, t).wait_send()

            @pl.when(z == entry(t, d))
            def _():
                r_last(kind, t, "wait")

    def stat_copy(name, k):
        return remote(
            name.out,
            name.slots.at[g],
            name.send.at[k],
            name.recv.at[k],
            (s, d, (g + k) % GRID),
        )

    lane = lax.broadcasted_iota(jnp.int32, (SEQ, HEAD), 1)

    def stat_start(name, first, second):
        both = jnp.where(lane == 0, first, jnp.where(lane == 1, second, 0.0))
        turned = both.T[0:8]
        name.out[...] = turned
        name.slots[g] = turned
        for k in range(1, GRID):
            stat_copy(name, k).start()

    def stat_finish(name):
        slots = name.slots
        for k in range(1, GRID):
            slot = slots.at[(g + GRID - k) % GRID]
            remote(
                slot, slot, name.send.at[k], name.recv.at[k], sibling
            ).wait_recv()
        total = jnp.sum(slots[...], axis=0)
        padded = jnp.concatenate([total, jnp.zeros((HEAD - 8, SEQ), F32)], axis=0)
        columns = padded.T
        return columns[:, 0:1], columns[:, 1:2]

    def stat_drain(name):
        for k in range(1, GRID):
            stat_copy(name, k).wait_send()

    def small_copy(name, k):
        return remote(
            name.out,
            name.slots.at[d],
            name.send.at[k],
            name.recv.at[k],
            at((d + k) % 4, z, x, c),
        )

    def small_start(name):
        name.slots[d] = name.out[...]
        for k in range(1, 4):
            small_copy(name, k).start()

    def small_finish(name):
        slots = name.slots
        for k in range(1, 4):
            slot = slots.at[(d + 4 - k) % 4]
            remote(
                slot, slot, name.send.at[k], name.recv.at[k], above
            ).wait_recv()
        return jnp.sum(slots[...], axis=0)

    def small_drain(name):
        for k in range(1, 4):
            small_copy(name, k).wait_send()

    xs = (buf.big_x, acts)
    cs = (buf.big_c, cots)
    xw = (0, QKV)
    cw = (QKV, 256)
    own_send(cot_ref.at[0], buf.big_c, cots)
    values = x_ref[0].astype(F32)
    stat_start(
        stat_a,
        jnp.sum(values, axis=-1, keepdims=True),
        jnp.sum(values * values, axis=-1, keepdims=True),
    )
    first, second = stat_finish(stat_a)
    width = 4 * ROWS
    centre = first / width
    reciprocal = lax.rsqrt(second / width - centre * centre + EPSILON)
    gain = ng_ref[...].astype(F32)
    centred = (x_ref[0].astype(F32) - centre) * reciprocal
    buf.centred[...] = centred
    buf.recip[...] = jnp.broadcast_to(reciprocal, (SEQ, HEAD))
    buf.norm[...] = (centred * gain).astype(BF16)
    near_step(*cs, up)
    near_step(*cs, down)
    near_step(*cs, across)
    near_step(*cs, d)
    own_send(buf.norm, buf.big_x, acts)
    side_step(*cs, up)
    side_step(*cs, down)
    far_step(*cs, up)
    near_step(*xs, across)
    far_step(*cs, down)
    side_step(*cs, across)
    w_copy.wait()
    multiply_step(*cs, *cw, 1)
    far_step(*cs, across)
    side_step(*xs, across)
    multiply_step(*cs, *cw, 3)
    multiply_step(*cs, *cw, 2)
    side_step(*cs, d)
    near_step(*xs, up)
    far_step(*xs, across)
    near_step(*xs, down)
    multiply_step(*xs, *xw, 2)
    side_sent(*cs, down)
    side_step(*xs, down)
    pass_on(cots, *cw, 0, 0)
    far_step(*cs, d)
    near_step(*xs, d)
    side_step(*xs, up)
    pass_on(cots, *cw, 1, 1)
    multiply_step(*cs, *cw, 0)
    far_step(*xs, down)
    multiply_step(*xs, *xw, 3)
    far_step(*xs, up)
    multiply_step(*xs, *xw, 1)
    side_step(*xs, d)
    pass_on(acts, *xw, 0, 0)
    pass_on(acts, *xw, 1, 1)
    far_step(*xs, d)
    side_sent(*cs, across)
    multiply_step(*xs, *xw, 0)
    finish_depth(cots, *cw)
    finish_depth(acts, *xw)
    own = buf.own_acc
    for h in range(2):
        cols = [slice(part * 256 + h * HEAD, part * 256 + (h + 1) * HEAD) for part in range(4)]
        for part in range(2):
            hat, rec = normalize(own[:, cols[part]])
            buf.hats[2 * part + h] = hat
            buf.recs[2 * part + h] = jnp.broadcast_to(rec, (SEQ, HEAD))
            row = hg_ref[0, part, h : h + 1, :].astype(F32)
            buf.lows[2 * part + h] = (hat * row).astype(BF16)
        buf.lows[4 + h] = own[:, cols[2]].astype(BF16)
        scores = dot_nt(buf.lows[h], buf.lows[2 + h]) * SCALE
        exponent = jnp.exp(scores)
        attention = exponent / jnp.sum(exponent, axis=-1, keepdims=True)
        buf.attention[h] = attention
        attended = dot(attention.astype(BF16), buf.lows[4 + h])
        buf.att[tokens(d), h * HEAD : (h + 1) * HEAD] = attended.astype(BF16)
    gains.out[...] = jnp.zeros((8, HEAD), F32)
    for h in range(2):
        d_attended = own[:, QKV + h * HEAD : QKV + (h + 1) * HEAD].astype(BF16)
        attention = buf.attention[h]
        d_attention = dot_nt(d_attended, buf.lows[4 + h])
        row_delta = jnp.sum(attention * d_attention, axis=-1, keepdims=True)
        d_score = (attention * (d_attention - row_delta) * SCALE).astype(BF16)
        d_query = dot(d_score, buf.lows[2 + h])
        d_key = dot_tn(d_score, buf.lows[h])
        d_value = dot_tn(attention.astype(BF16), d_attended)
        for part, upstream in enumerate((d_query, d_key)):
            hat = buf.hats[2 * part + h]
            row = hg_ref[0, part, h : h + 1, :].astype(F32)
            grad = normalize_back(upstream, hat, buf.recs[2 * part + h][:, 0:1], row)
            at_col = part * 256 + h * HEAD
            buf.dp[tokens(d), at_col : at_col + HEAD] = grad.astype(BF16)
            index = 2 * part + h
            gains.out[index : index + 1, :] = jnp.sum(upstream * hat, axis=0, keepdims=True)
        at_col = 512 + h * HEAD
        buf.dp[tokens(d), at_col : at_col + HEAD] = d_value.astype(BF16)
    small_start(gains)
    ring_start(buf.dp, acts)
    ring_start(buf.att, cots)
    first_stage(buf.att, branch, QKV, d)
    ring_more(buf.att, cots)
    second_stage(branch, d)
    ring_forward(buf.att, cots)
    ring_more(buf.dp, acts)
    third_stage(branch, d)
    first_stage(buf.dp, inputs, 0, d)
    ring_near(buf.att, cots)
    first_stage(buf.att, branch, QKV, down)
    first_stage(buf.att, branch, QKV, up)
    ring_far(buf.att, cots)
    side_sent(*xs, up)
    second_stage(branch, up)
    second_stage(inputs, d)
    third_stage(branch, up)
    fourth_stage(branch, d)
    second_stage(branch, down)
    ring_forward(buf.dp, acts)
    first_stage(buf.att, branch, QKV, across)
    second_stage(branch, across)
    third_stage(inputs, d)
    ring_near(buf.dp, acts)
    fourth_stage(branch, up)
    first_stage(buf.dp, inputs, 0, up)
    side_done(inputs, d)
    first_stage(buf.dp, inputs, 0, down)
    third_stage(branch, across)
    side_done(branch, up)
    side_done(branch, across)
    side_sent(*cs, up)
    third_stage(branch, down)
    second_stage(inputs, down)
    second_stage(inputs, up)
    fourth_stage(branch, across)
    ring_far(buf.dp, acts)
    first_stage(buf.dp, inputs, 0, across)
    third_stage(inputs, up)
    fourth_stage(branch, down)
    side_done(branch, down)
    second_stage(inputs, across)
    third_stage(inputs, down)
    fourth_stage(inputs, up)
    side_sent(*cs, d)
    third_stage(inputs, across)
    fourth_stage(inputs, down)
    side_done(inputs, across)
    fourth_stage(inputs, across)
    fourth_stage(inputs, d)
    side_done(branch, d)
    side_done(inputs, down)

    def weight_rows(k, _):
        rows = pl.ds(pl.multiple_of(k * 256, 256), 256)
        dw_ref[rows, 0:QKV] = dot_tn(buf.big_x[:, rows], buf.dp[...]).astype(BF16)
        dw_ref[rows, QKV:COLS] = dot_tn(buf.big_c[:, rows], buf.att[...]).astype(BF16)
        return 0

    lax.fori_loop(0, 6, weight_rows, 0)

    side_sent(*xs, across)
    side_done(inputs, up)
    side_sent(*xs, d)
    d_normed = last_stage(inputs)
    weighted = d_normed * gain
    centred = buf.centred[...]
    stat_start(
        stat_b,
        jnp.sum(weighted, axis=-1, keepdims=True),
        jnp.sum(weighted * centred, axis=-1, keepdims=True),
    )
    norms.out[...] = jnp.broadcast_to(
        jnp.sum(d_normed * centred, axis=0, keepdims=True), (8, FEATURES)
    )
    small_start(norms)
    total = small_finish(gains)
    for part in range(2):
        hgg_ref[0, part] = total[2 * part : 2 * part + 2]
    first, second = stat_finish(stat_b)
    reciprocal = buf.recip[:, 0:1]
    grad = reciprocal * (weighted - first / width - centred * (second / width))
    buf.grad_out[...] = grad.astype(BF16)
    grad_copy = remote(
        buf.grad_out,
        buf.grad_in,
        sems.grad_send.at[0],
        sems.grad_recv.at[0],
        (section_down, d, g),
    )
    grad_copy.start()
    ngg_ref[...] = small_finish(norms)[0:1]
    drain_gather(cot_ref.at[0], buf.big_c, cots)
    drain_gather(buf.norm, buf.big_x, acts)
    drain_depth(acts, 0, QKV)
    drain_depth(cots, QKV, 256)
    for step in range(4, 6):
        ring_copy(buf.att, cots, step).wait_send()
        ring_copy(buf.dp, acts, step).wait_send()
    fifth_stage(branch, across)
    fifth_stage(branch, up)
    side_sent(*xs, down)
    fifth_stage(branch, down)
    fifth_stage(branch, d)
    nb_ref[0] = last_stage(branch).astype(BF16)
    drain_reduce(branch)
    drain_reduce(inputs)
    stat_drain(stat_a)
    stat_drain(stat_b)
    small_drain(gains)
    small_drain(norms)
    grad_copy.wait()
    rg_ref[0] = buf.grad_in[...]


def local(section_input, cotangent, projections, norm_gain, head_gains):
    weights = projections.reshape(ROWS, COLS)
    here = pl.BlockSpec(memory_space=pltpu.VMEM)
    outs = pl.pallas_call(
        kernel,
        out_shape=(
            jax.ShapeDtypeStruct((1, SEQ, FEATURES), BF16),
            jax.ShapeDtypeStruct((1, SEQ, FEATURES), BF16),
            jax.ShapeDtypeStruct((ROWS, COLS), BF16),
            jax.ShapeDtypeStruct((1, FEATURES), F32),
            jax.ShapeDtypeStruct((1, 2, 2, HEAD), F32),
        ),
        in_specs=[here, here, pl.BlockSpec(memory_space=pl.ANY), here, here],
        out_specs=(here,) * 5,
        scratch_shapes=LEAVES,
        compiler_params=pltpu.CompilerParams(
            collective_id=0, has_side_effects=True, vmem_limit_bytes=60 * 1024 * 1024
        ),
        name="block",
    )(section_input, cotangent, weights, norm_gain, head_gains)
    next_branch, returned, weight_grad, norm_total, head_total = outs
    return (
        next_branch,
        returned,
        weight_grad.reshape(1, ROWS, 4, 256),
        norm_total,
        head_total,
    )


def solution(mesh):
    in_specs = (
        P("section", "depth", "grid"),
        P("section", "depth", "grid"),
        P("section", "depth", None, "grid"),
        P("section", "grid"),
        P("section", None, "grid", None),
    )
    out_specs = (
        P("section", "depth", "grid"),
        P("section", "depth", "grid"),
        P("section", "depth", None, "grid"),
        P("section", "grid"),
        P("section", None, "grid", None),
    )
    return jax.shard_map(local, mesh=mesh, in_specs=in_specs, out_specs=out_specs, check_vma=False)
```

time: 674 us -> 192 us (0.28)
  waiting for transfers between devices: 371 us -> 0 us
  Pallas kernels: 0 us -> 178 us
  blocking collectives: 152 us -> 0 us
  local copies, waits for them, and re-layouts: 66.3 us -> 13 us
  matrix products: 34.8 us -> 0 us
  other arithmetic: 21.7 us -> 0 us
  between operations: 14.4 us -> 0.68 us
  starting transfers between devices: 12.9 us -> 0 us
    all_gather x4 -> x0, waiting for transfers between devices: 254 us -> none  [the longest x1 224 us: local(): weights = lax.all_gather(projections, 'depth', axis=1, tiled=True)[0]]
    pallas_call x0 -> x1, Pallas kernels: none -> 178 us  [local(): pl.pallas_call(kernel, out_shape=(jax.ShapeDtypeStruct((1, SEQ, FEATURES)...]
    all_gather x2 -> x0, blocking collectives: 111 us -> none  [the longest x1 92.2 us: local(): lax.all_gather(attended, 'depth', axis=0, tiled=True)]
    all_to_all x2 -> x0, waiting for transfers between devices: 71.1 us -> none  [the longest x1 71 us: local(): lax.all_to_all(full_cot, 'depth', split_axis=1, concat_axis=0, tiled=True)]
    unnamed x8 -> x0, waiting for transfers between devices: 46.6 us -> none
    psum x2 -> x0, blocking collectives: 41 us -> none  [the longest x1 28.6 us: local(): lax.psum((jnp.sum(weighted, axis=-1), jnp.sum(weighted * own_centred, axi...]
    dot_general x12 -> x0, matrix products: 34.5 us -> none  [the longest x1 8.06 us: local(): jnp.einsum('tck,dck->td', d_project, weights[:, :3], preferred_element_ty...]
    unnamed x39 -> x13, local copies, waits for them, and re-layouts: 36 us -> 6.82 us
  transfers between devices with their start and end apart: 10 -> 0, of which waited for: 5 -> 0; matrix products, arithmetic and copies ran while one was open for 16% -> 0% of each run, Pallas kernels for 0% -> 0%
where the time goes in v1:
time: 192 us
  Pallas kernels  178 us (93%)
  local copies, waits for them, and re-layouts  13 us (7%)
    pallas_call x1, Pallas kernels, local(): pl.pallas_call(kernel, out_shape=(jax.ShapeDtypeStruct((1, SEQ, FEATURES)...  178 us
    unnamed x13, local copies, waits for them, and re-layouts  6.82 us
    reshape x1, local copies, waits for them, and re-layouts, local(): weight_grad.reshape(1, ROWS, 4, 256)  6.22 us

profile of v1, /device:TPU:32, one launch (start us, length us, event | category | flops | bytes accessed | tf_op | source)
XLA Modules:
  0.0 192.0 jit_solution(7951347600309132731)
XLA Ops:
  0.6 4.3 %copy.10 = bf16[192,8,4,256]{3,1,2,0:T(8,128)(2,1)} copy(bf16[192,8,4,256]{3,2,1,0:T(4,128)(2,1)} %bitcast.4) | data formatting | bytes 6291456
  4.9 178.3 %block.1 = (bf16[1,256,384]{2,1,0:T(8,128)(2,1)}, bf16[1,256,384]{2,1,0:T(8,128)(2,1)}, bf16[1536,1024]{1,0:T(8,128)(2,1)}, f32[1,384]{1,0:T(1,128)}, f32[1,2,2,128]{3,2,1,0:T(2,128)}) custom-call(bf16[1,256,384]{2,1,0:T(8,128)(2,1)} %refs_0_.1, bf16[1,256,384]{2,1,0:T(8,128)(2,1)} %refs_1_.1, bf16[1536,1024]{1,0:T(8,128)(2,1)} %bitcast.3, ...), custom_call_target="tpu_custom_call" | custom-call | tf_op jit(solution)/shard_map/block/pallas_call | solution.py:902
  183.3 0.0 copy-start.1
  183.3 0.0 copy-start
  183.3 0.0 copy-start.3
  183.3 0.0 copy-start.2
  183.3 6.2 %reshape.17 = bf16[1,1536,4,256]{3,2,1,0:T(4,128)(2,1)} reshape(bf16[1536,1024]{1,0:T(8,128)(2,1)} %get-tuple-element.12) | data formatting | bytes 6291456 | tf_op jit(solution)/shard_map/reshape | solution.py:923
  189.5 0.0 copy-done.1
  189.5 0.7 copy.15
  190.2 0.0 copy-done
  190.2 0.7 copy.16
  190.9 0.0 copy-done.3
  190.9 0.6 copy.17
  191.5 0.0 copy-done.2
  191.5 0.6 copy.18
Async XLA Ops:
  183.3 6.3 %copy-start.1 = (bf16[1,256,384]{2,1,0:T(8,128)(2,1)S(1)}, bf16[1,256,384]{2,1,0:T(8,128)(2,1)}, u32[]{:S(2)}) copy-start(bf16[1,256,384]{2,1,0:T(8,128)(2,1)} %get-tuple-element.20) | copy-start | bytes 589828
  183.3 6.9 %copy-start = (bf16[1,256,384]{2,1,0:T(8,128)(2,1)S(1)}, bf16[1,256,384]{2,1,0:T(8,128)(2,1)}, u32[]{:S(2)}) copy-start(bf16[1,256,384]{2,1,0:T(8,128)(2,1)} %get-tuple-element.21) | copy-start | bytes 589828
  183.3 7.6 %copy-start.3 = (f32[1,384]{1,0:T(1,128)S(1)}, f32[1,384]{1,0:T(1,128)}, u32[]{:S(2)}) copy-start(f32[1,384]{1,0:T(1,128)} %get-tuple-element.23) | copy-start | bytes 4612
  183.3 8.2 %copy-start.2 = (f32[1,2,2,128]{3,2,1,0:T(2,128)S(1)}, f32[1,2,2,128]{3,2,1,0:T(2,128)}, u32[]{:S(2)}) copy-start(f32[1,2,2,128]{3,2,1,0:T(2,128)} %get-tuple-element.24) | copy-start | bytes 6148

commit v2 on v1

--- a/solution.py
+++ b/solution.py
@@ -133,6 +133,7 @@
     sems=dict(w=dma(1), grad_send=dma(1), grad_recv=dma(1)),
     buf=dict(
         w=vmem((ROWS, COLS), BF16),
+        raw=vmem((ROWS, 4, 256), BF16),
         norm=vmem((SEQ, FEATURES), BF16),
         centred=vmem((SEQ, FEATURES), F32),
         recip=vmem((SEQ, HEAD), F32),
@@ -232,7 +233,7 @@
 
     pl.semaphore_wait(barrier, 26 + 4 * (((home - d + 4) % 4 + 3) // 4))
 
-    w_copy = pltpu.make_async_copy(w_hbm, w, sems.w.at[0])
+    w_copy = pltpu.make_async_copy(w_hbm.at[0], buf.raw, sems.w.at[0])
     w_copy.start()
 
     def tokens(t):
@@ -686,6 +687,25 @@
     cs = (buf.big_c, cots)
     xw = (0, QKV)
     cw = (QKV, 256)
+    def weight_qkv(k):
+        rows = slice(k * 256, (k + 1) * 256)
+        dw_ref[rows, 0:QKV] = dot_tn(buf.big_x[:, rows], buf.dp[...]).astype(BF16)
+
+    def weight_out(k):
+        rows = slice(k * 256, (k + 1) * 256)
+        dw_ref[rows, QKV:COLS] = dot_tn(buf.big_c[:, rows], buf.att[...]).astype(BF16)
+
+    def relayout(k, _):
+        rows = pl.ds(pl.multiple_of(k * 128, 128), 128)
+        chunk = buf.raw[rows]
+        for part in range(4):
+            w[rows, part * 256 : (part + 1) * 256] = chunk[:, part, :]
+        return 0
+
+    def relayout_all():
+        w_copy.wait()
+        lax.fori_loop(0, ROWS // 128, relayout, 0)
+
     own_send(cot_ref.at[0], buf.big_c, cots)
     values = x_ref[0].astype(F32)
     stat_start(
@@ -693,6 +713,7 @@
         jnp.sum(values, axis=-1, keepdims=True),
         jnp.sum(values * values, axis=-1, keepdims=True),
     )
+    relayout_all()
     first, second = stat_finish(stat_a)
     width = 4 * ROWS
     centre = first / width
@@ -702,47 +723,45 @@
     buf.centred[...] = centred
     buf.recip[...] = jnp.broadcast_to(reciprocal, (SEQ, HEAD))
     buf.norm[...] = (centred * gain).astype(BF16)
-    near_step(*cs, up)
     near_step(*cs, down)
     near_step(*cs, across)
+    own_send(buf.norm, buf.big_x, acts)
+    near_step(*cs, up)
+    side_step(*cs, down)
+    side_step(*cs, across)
     near_step(*cs, d)
-    own_send(buf.norm, buf.big_x, acts)
     side_step(*cs, up)
-    side_step(*cs, down)
+    far_step(*cs, across)
+    near_step(*xs, across)
+    multiply_step(*cs, *cw, 2)
+    near_step(*xs, up)
+    side_step(*xs, across)
     far_step(*cs, up)
-    near_step(*xs, across)
+    near_step(*xs, down)
     far_step(*cs, down)
-    side_step(*cs, across)
-    w_copy.wait()
+    near_step(*xs, d)
+    far_step(*xs, across)
+    multiply_step(*cs, *cw, 3)
+    multiply_step(*xs, *xw, 2)
+    side_step(*xs, down)
+    side_step(*cs, d)
+    side_sent(*xs, up)
     multiply_step(*cs, *cw, 1)
-    far_step(*cs, across)
-    side_step(*xs, across)
-    multiply_step(*cs, *cw, 3)
-    multiply_step(*cs, *cw, 2)
-    side_step(*cs, d)
-    near_step(*xs, up)
-    far_step(*xs, across)
-    near_step(*xs, down)
-    multiply_step(*xs, *xw, 2)
-    side_sent(*cs, down)
-    side_step(*xs, down)
-    pass_on(cots, *cw, 0, 0)
+    side_step(*xs, d)
+    side_step(*xs, up)
     far_step(*cs, d)
-    near_step(*xs, d)
-    side_step(*xs, up)
-    pass_on(cots, *cw, 1, 1)
-    multiply_step(*cs, *cw, 0)
+    far_step(*xs, up)
     far_step(*xs, down)
     multiply_step(*xs, *xw, 3)
-    far_step(*xs, up)
+    side_sent(*cs, down)
+    pass_on(cots, *cw, 0, 0)
     multiply_step(*xs, *xw, 1)
-    side_step(*xs, d)
+    multiply_step(*cs, *cw, 0)
+    far_step(*xs, d)
+    pass_on(acts, *xw, 1, 1)
+    pass_on(cots, *cw, 1, 1)
+    multiply_step(*xs, *xw, 0)
     pass_on(acts, *xw, 0, 0)
-    pass_on(acts, *xw, 1, 1)
-    far_step(*xs, d)
-    side_sent(*cs, across)
-    multiply_step(*xs, *xw, 0)
-    finish_depth(cots, *cw)
     finish_depth(acts, *xw)
     own = buf.own_acc
     for h in range(2):
@@ -760,6 +779,9 @@
         buf.attention[h] = attention
         attended = dot(attention.astype(BF16), buf.lows[4 + h])
         buf.att[tokens(d), h * HEAD : (h + 1) * HEAD] = attended.astype(BF16)
+    ring_start(buf.att, cots)
+    ring_more(buf.att, cots)
+    finish_depth(cots, *cw)
     gains.out[...] = jnp.zeros((8, HEAD), F32)
     for h in range(2):
         d_attended = own[:, QKV + h * HEAD : QKV + (h + 1) * HEAD].astype(BF16)
@@ -781,70 +803,73 @@
         at_col = 512 + h * HEAD
         buf.dp[tokens(d), at_col : at_col + HEAD] = d_value.astype(BF16)
     small_start(gains)
+    first_stage(buf.att, branch, QKV, d)
     ring_start(buf.dp, acts)
-    ring_start(buf.att, cots)
-    first_stage(buf.att, branch, QKV, d)
-    ring_more(buf.att, cots)
     second_stage(branch, d)
     ring_forward(buf.att, cots)
-    ring_more(buf.dp, acts)
-    third_stage(branch, d)
     first_stage(buf.dp, inputs, 0, d)
     ring_near(buf.att, cots)
     first_stage(buf.att, branch, QKV, down)
     first_stage(buf.att, branch, QKV, up)
+    second_stage(branch, down)
+    ring_more(buf.dp, acts)
+    second_stage(branch, up)
+    third_stage(branch, down)
+    third_stage(branch, up)
     ring_far(buf.att, cots)
-    side_sent(*xs, up)
-    second_stage(branch, up)
+    side_sent(*xs, across)
     second_stage(inputs, d)
-    third_stage(branch, up)
-    fourth_stage(branch, d)
-    second_stage(branch, down)
+    third_stage(branch, d)
+    first_stage(buf.att, branch, QKV, across)
+    fourth_stage(branch, down)
+    side_sent(*xs, down)
+    side_done(branch, up)
     ring_forward(buf.dp, acts)
-    first_stage(buf.att, branch, QKV, across)
+    ring_near(buf.dp, acts)
     second_stage(branch, across)
-    third_stage(inputs, d)
-    ring_near(buf.dp, acts)
+    side_done(branch, d)
     fourth_stage(branch, up)
     first_stage(buf.dp, inputs, 0, up)
-    side_done(inputs, d)
+    third_stage(inputs, d)
+    weight_out(5)
+    third_stage(branch, across)
+    second_stage(inputs, up)
     first_stage(buf.dp, inputs, 0, down)
-    third_stage(branch, across)
-    side_done(branch, up)
-    side_done(branch, across)
+    fifth_stage(branch, up)
+    fifth_stage(branch, down)
     side_sent(*cs, up)
-    third_stage(branch, down)
     second_stage(inputs, down)
-    second_stage(inputs, up)
-    fourth_stage(branch, across)
+    fourth_stage(branch, d)
+    weight_out(1)
+    third_stage(inputs, up)
+    third_stage(inputs, down)
+    weight_out(4)
     ring_far(buf.dp, acts)
     first_stage(buf.dp, inputs, 0, across)
-    third_stage(inputs, up)
-    fourth_stage(branch, down)
+    second_stage(inputs, across)
+    side_sent(*xs, d)
+    side_done(inputs, down)
+    fourth_stage(branch, across)
+    fifth_stage(branch, d)
+    weight_qkv(2)
+    fourth_stage(inputs, down)
+    side_done(inputs, up)
+    weight_qkv(1)
+    side_sent(*cs, across)
+    third_stage(inputs, across)
+    weight_qkv(0)
+    weight_out(0)
+    weight_out(3)
+    side_done(inputs, d)
+    fourth_stage(inputs, up)
+    weight_qkv(5)
+    side_sent(*cs, d)
+    weight_qkv(3)
+    side_done(inputs, across)
     side_done(branch, down)
-    second_stage(inputs, across)
-    third_stage(inputs, down)
-    fourth_stage(inputs, up)
-    side_sent(*cs, d)
-    third_stage(inputs, across)
-    fourth_stage(inputs, down)
-    side_done(inputs, across)
+    fourth_stage(inputs, d)
     fourth_stage(inputs, across)
-    fourth_stage(inputs, d)
-    side_done(branch, d)
-    side_done(inputs, down)
-
-    def weight_rows(k, _):
-        rows = pl.ds(pl.multiple_of(k * 256, 256), 256)
-        dw_ref[rows, 0:QKV] = dot_tn(buf.big_x[:, rows], buf.dp[...]).astype(BF16)
-        dw_ref[rows, QKV:COLS] = dot_tn(buf.big_c[:, rows], buf.att[...]).astype(BF16)
-        return 0
-
-    lax.fori_loop(0, 6, weight_rows, 0)
-
-    side_sent(*xs, across)
-    side_done(inputs, up)
-    side_sent(*xs, d)
+    weight_qkv(4)
     d_normed = last_stage(inputs)
     weighted = d_normed * gain
     centred = buf.centred[...]
@@ -881,10 +906,8 @@
         ring_copy(buf.att, cots, step).wait_send()
         ring_copy(buf.dp, acts, step).wait_send()
     fifth_stage(branch, across)
-    fifth_stage(branch, up)
-    side_sent(*xs, down)
-    fifth_stage(branch, down)
-    fifth_stage(branch, d)
+    side_done(branch, across)
+    weight_out(2)
     nb_ref[0] = last_stage(branch).astype(BF16)
     drain_reduce(branch)
     drain_reduce(inputs)
@@ -897,7 +920,6 @@
 
 
 def local(section_input, cotangent, projections, norm_gain, head_gains):
-    weights = projections.reshape(ROWS, COLS)
     here = pl.BlockSpec(memory_space=pltpu.VMEM)
     outs = pl.pallas_call(
         kernel,
@@ -915,7 +937,7 @@
             collective_id=0, has_side_effects=True, vmem_limit_bytes=60 * 1024 * 1024
         ),
         name="block",
-    )(section_input, cotangent, weights, norm_gain, head_gains)
+    )(section_input, cotangent, projections, norm_gain, head_gains)
     next_branch, returned, weight_grad, norm_total, head_total = outs
     return (
         next_branch,

time: 192 us -> 188 us (0.979)
  local copies, waits for them, and re-layouts: 13 us -> 8.74 us
    unnamed x13 -> x12, local copies, waits for them, and re-layouts: 6.82 us -> 2.51 us
where the time goes in v2:
time: 188 us
  Pallas kernels  178 us (95%)
  local copies, waits for them, and re-layouts  8.74 us (5%)
    pallas_call x1, Pallas kernels, local(): pl.pallas_call(kernel, out_shape=(jax.ShapeDtypeStruct((1, SEQ, FEATURES)...  178 us
    reshape x1, local copies, waits for them, and re-layouts, local(): weight_grad.reshape(1, ROWS, 4, 256)  6.22 us

profile of v2, /device:TPU:32, one launch (start us, length us, event | category | flops | bytes accessed | tf_op | source)
XLA Modules:
  0.0 187.6 jit_solution(10114118582451729580)
XLA Ops:
  0.6 178.2 %block.1 = (bf16[1,256,384]{2,1,0:T(8,128)(2,1)}, bf16[1,256,384]{2,1,0:T(8,128)(2,1)}, bf16[1536,1024]{1,0:T(8,128)(2,1)}, f32[1,384]{1,0:T(1,128)}, f32[1,2,2,128]{3,2,1,0:T(2,128)}) custom-call(bf16[1,256,384]{2,1,0:T(8,128)(2,1)} %refs_0_.1, bf16[1,256,384]{2,1,0:T(8,128)(2,1)} %refs_1_.1, bf16[1,1536,4,256]{3,2,1,0:T(4,128)(2,1)} %refs_2_.1, ...), custom_call_target="tpu_custom_call" | custom-call | tf_op jit(solution)/shard_map/block/pallas_call | solution.py:924
  178.8 0.0 copy-start.1
  178.8 0.0 copy-start
  178.9 0.0 copy-start.3
  178.9 0.0 copy-start.2
  178.9 6.2 %reshape.13 = bf16[1,1536,4,256]{3,2,1,0:T(4,128)(2,1)} reshape(bf16[1536,1024]{1,0:T(8,128)(2,1)} %get-tuple-element.12) | data formatting | bytes 6291456 | tf_op jit(solution)/shard_map/reshape | solution.py:945
  185.1 0.0 copy-done.1
  185.1 0.7 copy.14
  185.8 0.0 copy-done
  185.8 0.7 copy.15
  186.5 0.0 copy-done.3
  186.5 0.6 copy.16
  187.0 0.0 copy-done.2
  187.0 0.6 copy.17
Async XLA Ops:
  178.8 6.3 %copy-start.1 = (bf16[1,256,384]{2,1,0:T(8,128)(2,1)S(1)}, bf16[1,256,384]{2,1,0:T(8,128)(2,1)}, u32[]{:S(2)}) copy-start(bf16[1,256,384]{2,1,0:T(8,128)(2,1)} %get-tuple-element.20) | copy-start | bytes 589828
  178.8 6.9 %copy-start = (bf16[1,256,384]{2,1,0:T(8,128)(2,1)S(1)}, bf16[1,256,384]{2,1,0:T(8,128)(2,1)}, u32[]{:S(2)}) copy-start(bf16[1,256,384]{2,1,0:T(8,128)(2,1)} %get-tuple-element.21) | copy-start | bytes 589828
  178.9 7.6 %copy-start.3 = (f32[1,384]{1,0:T(1,128)S(1)}, f32[1,384]{1,0:T(1,128)}, u32[]{:S(2)}) copy-start(f32[1,384]{1,0:T(1,128)} %get-tuple-element.23) | copy-start | bytes 4612
  178.9 8.2 %copy-start.2 = (f32[1,2,2,128]{3,2,1,0:T(2,128)S(1)}, f32[1,2,2,128]{3,2,1,0:T(2,128)}, u32[]{:S(2)}) copy-start(f32[1,2,2,128]{3,2,1,0:T(2,128)} %get-tuple-element.24) | copy-start | bytes 6148

commit v3 on v2

--- a/solution.py
+++ b/solution.py
@@ -126,7 +126,8 @@
     cots=gather_scratch(),
     branch=reduce_scratch(),
     inputs=reduce_scratch(),
-    stat_a=sum_scratch(GRID, 8, SEQ),
+    stat_a=sum_scratch(GRID, 8, SEQ + FEATURES),
+    sums=sum_scratch(4, 8, QKV),
     stat_b=sum_scratch(GRID, 8, SEQ),
     gains=sum_scratch(4, 8, HEAD),
     norms=sum_scratch(4, 8, FEATURES),
@@ -168,7 +169,8 @@
     parts = jax.tree.unflatten(TREE, refs[10:])
     parts = {name: SimpleNamespace(**part) for name, part in parts.items()}
     acts, cots, branch, inputs = (parts[name] for name in ("acts", "cots", "branch", "inputs"))
-    stat_a, stat_b, gains, norms = (parts[name] for name in ("stat_a", "stat_b", "gains", "norms"))
+    stat_a, stat_b = parts["stat_a"], parts["stat_b"]
+    gains, norms, sums = parts["gains"], parts["norms"], parts["sums"]
     sems, buf = parts["sems"], parts["buf"]
     w = buf.w
 
@@ -635,8 +637,10 @@
     def stat_start(name, first, second):
         both = jnp.where(lane == 0, first, jnp.where(lane == 1, second, 0.0))
         turned = both.T[0:8]
-        name.out[...] = turned
-        name.slots[g] = turned
+        name.out[:, 0:SEQ] = turned
+        if name is stat_a:
+            name.out[:, SEQ:] = jnp.broadcast_to(ng_ref[...].astype(F32), (8, FEATURES))
+        name.slots[g] = name.out[...]
         for k in range(1, GRID):
             stat_copy(name, k).start()
 
@@ -647,7 +651,7 @@
             remote(
                 slot, slot, name.send.at[k], name.recv.at[k], sibling
             ).wait_recv()
-        total = jnp.sum(slots[...], axis=0)
+        total = jnp.sum(slots[:, :, 0:SEQ], axis=0)
         padded = jnp.concatenate([total, jnp.zeros((HEAD - 8, SEQ), F32)], axis=0)
         columns = padded.T
         return columns[:, 0:1], columns[:, 1:2]
@@ -726,6 +730,12 @@
     near_step(*cs, down)
     near_step(*cs, across)
     own_send(buf.norm, buf.big_x, acts)
+    gain_rows = jnp.zeros((8, QKV), F32)
+    for j in range(4):
+        row = stat_a.slots[4 * d + j, :, SEQ:].astype(BF16)
+        gain_rows = gain_rows + dot(row, w[j * FEATURES : (j + 1) * FEATURES, 0:QKV])
+    sums.out[...] = gain_rows
+    small_start(sums)
     near_step(*cs, up)
     side_step(*cs, down)
     side_step(*cs, across)
@@ -783,6 +793,9 @@
     ring_more(buf.att, cots)
     finish_depth(cots, *cw)
     gains.out[...] = jnp.zeros((8, HEAD), F32)
+    gain_row = small_finish(sums)[0:1]
+    firsts = jnp.zeros((SEQ, HEAD), F32)
+    seconds = jnp.zeros((SEQ, HEAD), F32)
     for h in range(2):
         d_attended = own[:, QKV + h * HEAD : QKV + (h + 1) * HEAD].astype(BF16)
         attention = buf.attention[h]
@@ -797,14 +810,25 @@
             row = hg_ref[0, part, h : h + 1, :].astype(F32)
             grad = normalize_back(upstream, hat, buf.recs[2 * part + h][:, 0:1], row)
             at_col = part * 256 + h * HEAD
-            buf.dp[tokens(d), at_col : at_col + HEAD] = grad.astype(BF16)
+            low = grad.astype(BF16)
+            buf.dp[tokens(d), at_col : at_col + HEAD] = low
+            firsts = firsts + low.astype(F32) * gain_row[:, at_col : at_col + HEAD]
+            seconds = seconds + low.astype(F32) * own[:, at_col : at_col + HEAD]
             index = 2 * part + h
             gains.out[index : index + 1, :] = jnp.sum(upstream * hat, axis=0, keepdims=True)
         at_col = 512 + h * HEAD
-        buf.dp[tokens(d), at_col : at_col + HEAD] = d_value.astype(BF16)
+        low = d_value.astype(BF16)
+        buf.dp[tokens(d), at_col : at_col + HEAD] = low
+        firsts = firsts + low.astype(F32) * gain_row[:, at_col : at_col + HEAD]
+        seconds = seconds + low.astype(F32) * own[:, at_col : at_col + HEAD]
     small_start(gains)
     first_stage(buf.att, branch, QKV, d)
     ring_start(buf.dp, acts)
+    stat_start(
+        stat_b,
+        jnp.sum(firsts, axis=-1, keepdims=True),
+        jnp.sum(seconds, axis=-1, keepdims=True),
+    )
     second_stage(branch, d)
     ring_forward(buf.att, cots)
     first_stage(buf.dp, inputs, 0, d)
@@ -870,23 +894,11 @@
     fourth_stage(inputs, d)
     fourth_stage(inputs, across)
     weight_qkv(4)
+    first, second = stat_finish(stat_b)
+    reciprocal = buf.recip[:, 0:1]
+    centred = buf.centred[...]
     d_normed = last_stage(inputs)
     weighted = d_normed * gain
-    centred = buf.centred[...]
-    stat_start(
-        stat_b,
-        jnp.sum(weighted, axis=-1, keepdims=True),
-        jnp.sum(weighted * centred, axis=-1, keepdims=True),
-    )
-    norms.out[...] = jnp.broadcast_to(
-        jnp.sum(d_normed * centred, axis=0, keepdims=True), (8, FEATURES)
-    )
-    small_start(norms)
-    total = small_finish(gains)
-    for part in range(2):
-        hgg_ref[0, part] = total[2 * part : 2 * part + 2]
-    first, second = stat_finish(stat_b)
-    reciprocal = buf.recip[:, 0:1]
     grad = reciprocal * (weighted - first / width - centred * (second / width))
     buf.grad_out[...] = grad.astype(BF16)
     grad_copy = remote(
@@ -897,7 +909,13 @@
         (section_down, d, g),
     )
     grad_copy.start()
-    ngg_ref[...] = small_finish(norms)[0:1]
+    norms.out[...] = jnp.broadcast_to(
+        jnp.sum(d_normed * centred, axis=0, keepdims=True), (8, FEATURES)
+    )
+    small_start(norms)
+    total = small_finish(gains)
+    for part in range(2):
+        hgg_ref[0, part] = total[2 * part : 2 * part + 2]
     drain_gather(cot_ref.at[0], buf.big_c, cots)
     drain_gather(buf.norm, buf.big_x, acts)
     drain_depth(acts, 0, QKV)
@@ -914,7 +932,9 @@
     stat_drain(stat_a)
     stat_drain(stat_b)
     small_drain(gains)
+    small_drain(sums)
     small_drain(norms)
+    ngg_ref[...] = small_finish(norms)[0:1]
     grad_copy.wait()
     rg_ref[0] = buf.grad_in[...]
 

time: 188 us -> 189 us (level)
  no operation moved by 1% of the time
where the time goes in v3:
time: 189 us; the launch traced here: 188 us
  Pallas kernels  179 us (95%)
  local copies, waits for them, and re-layouts  8.74 us (5%)
    pallas_call x1, Pallas kernels, local(): pl.pallas_call(kernel, out_shape=(jax.ShapeDtypeStruct((1, SEQ, FEATURES)...  179 us
    reshape x1, local copies, waits for them, and re-layouts, local(): weight_grad.reshape(1, ROWS, 4, 256)  6.22 us

profile of v3, /device:TPU:32, one launch (start us, length us, event | category | flops | bytes accessed | tf_op | source)
XLA Modules:
  0.0 188.2 jit_solution(7371444248071833608)
XLA Ops:
  0.6 178.8 %block.1 = (bf16[1,256,384]{2,1,0:T(8,128)(2,1)}, bf16[1,256,384]{2,1,0:T(8,128)(2,1)}, bf16[1536,1024]{1,0:T(8,128)(2,1)}, f32[1,384]{1,0:T(1,128)}, f32[1,2,2,128]{3,2,1,0:T(2,128)}) custom-call(bf16[1,256,384]{2,1,0:T(8,128)(2,1)} %refs_0_.1, bf16[1,256,384]{2,1,0:T(8,128)(2,1)} %refs_1_.1, bf16[1,1536,4,256]{3,2,1,0:T(4,128)(2,1)} %refs_2_.1, ...), custom_call_target="tpu_custom_call" | custom-call | tf_op jit(solution)/shard_map/block/pallas_call | solution.py:944
  179.4 0.0 copy-start.1
  179.4 0.0 copy-start
  179.4 0.0 copy-start.3
  179.4 0.0 copy-start.2
  179.4 6.2 %reshape.13 = bf16[1,1536,4,256]{3,2,1,0:T(4,128)(2,1)} reshape(bf16[1536,1024]{1,0:T(8,128)(2,1)} %get-tuple-element.12) | data formatting | bytes 6291456 | tf_op jit(solution)/shard_map/reshape | solution.py:965
  185.7 0.0 copy-done.1
  185.7 0.7 copy.14
  186.3 0.0 copy-done
  186.3 0.7 copy.15
  187.0 0.0 copy-done.3
  187.0 0.6 copy.16
  187.6 0.0 copy-done.2
  187.6 0.6 copy.17
Async XLA Ops:
  179.4 6.3 %copy-start.1 = (bf16[1,256,384]{2,1,0:T(8,128)(2,1)S(1)}, bf16[1,256,384]{2,1,0:T(8,128)(2,1)}, u32[]{:S(2)}) copy-start(bf16[1,256,384]{2,1,0:T(8,128)(2,1)} %get-tuple-element.20) | copy-start | bytes 589828
  179.4 6.9 %copy-start = (bf16[1,256,384]{2,1,0:T(8,128)(2,1)S(1)}, bf16[1,256,384]{2,1,0:T(8,128)(2,1)}, u32[]{:S(2)}) copy-start(bf16[1,256,384]{2,1,0:T(8,128)(2,1)} %get-tuple-element.21) | copy-start | bytes 589828
  179.4 7.6 %copy-start.3 = (f32[1,384]{1,0:T(1,128)S(1)}, f32[1,384]{1,0:T(1,128)}, u32[]{:S(2)}) copy-start(f32[1,384]{1,0:T(1,128)} %get-tuple-element.23) | copy-start | bytes 4612
  179.4 8.2 %copy-start.2 = (f32[1,2,2,128]{3,2,1,0:T(2,128)S(1)}, f32[1,2,2,128]{3,2,1,0:T(2,128)}, u32[]{:S(2)}) copy-start(f32[1,2,2,128]{3,2,1,0:T(2,128)} %get-tuple-element.24) | copy-start | bytes 6148

commit v4 on v3

--- a/solution.py
+++ b/solution.py
@@ -750,26 +750,25 @@
     near_step(*xs, down)
     far_step(*cs, down)
     near_step(*xs, d)
+    multiply_step(*cs, *cw, 1)
     far_step(*xs, across)
     multiply_step(*cs, *cw, 3)
     multiply_step(*xs, *xw, 2)
     side_step(*xs, down)
+    side_sent(*xs, up)
     side_step(*cs, d)
-    side_sent(*xs, up)
-    multiply_step(*cs, *cw, 1)
     side_step(*xs, d)
     side_step(*xs, up)
     far_step(*cs, d)
+    far_step(*xs, down)
     far_step(*xs, up)
-    far_step(*xs, down)
     multiply_step(*xs, *xw, 3)
-    side_sent(*cs, down)
     pass_on(cots, *cw, 0, 0)
     multiply_step(*xs, *xw, 1)
     multiply_step(*cs, *cw, 0)
+    pass_on(cots, *cw, 1, 1)
     far_step(*xs, d)
     pass_on(acts, *xw, 1, 1)
-    pass_on(cots, *cw, 1, 1)
     multiply_step(*xs, *xw, 0)
     pass_on(acts, *xw, 0, 0)
     finish_depth(acts, *xw)
@@ -789,6 +788,7 @@
         buf.attention[h] = attention
         attended = dot(attention.astype(BF16), buf.lows[4 + h])
         buf.att[tokens(d), h * HEAD : (h + 1) * HEAD] = attended.astype(BF16)
+    side_sent(*cs, down)
     ring_start(buf.att, cots)
     ring_more(buf.att, cots)
     finish_depth(cots, *cw)
@@ -824,12 +824,12 @@
     small_start(gains)
     first_stage(buf.att, branch, QKV, d)
     ring_start(buf.dp, acts)
+    second_stage(branch, d)
     stat_start(
         stat_b,
         jnp.sum(firsts, axis=-1, keepdims=True),
         jnp.sum(seconds, axis=-1, keepdims=True),
     )
-    second_stage(branch, d)
     ring_forward(buf.att, cots)
     first_stage(buf.dp, inputs, 0, d)
     ring_near(buf.att, cots)
@@ -841,11 +841,12 @@
     third_stage(branch, down)
     third_stage(branch, up)
     ring_far(buf.att, cots)
-    side_sent(*xs, across)
     second_stage(inputs, d)
     third_stage(branch, d)
+    side_sent(*xs, across)
     first_stage(buf.att, branch, QKV, across)
     fourth_stage(branch, down)
+    weight_out(5)
     side_sent(*xs, down)
     side_done(branch, up)
     ring_forward(buf.dp, acts)
@@ -855,14 +856,13 @@
     fourth_stage(branch, up)
     first_stage(buf.dp, inputs, 0, up)
     third_stage(inputs, d)
-    weight_out(5)
     third_stage(branch, across)
     second_stage(inputs, up)
+    fifth_stage(branch, down)
     first_stage(buf.dp, inputs, 0, down)
+    second_stage(inputs, down)
     fifth_stage(branch, up)
-    fifth_stage(branch, down)
     side_sent(*cs, up)
-    second_stage(inputs, down)
     fourth_stage(branch, d)
     weight_out(1)
     third_stage(inputs, up)
@@ -870,30 +870,33 @@
     weight_out(4)
     ring_far(buf.dp, acts)
     first_stage(buf.dp, inputs, 0, across)
+    weight_qkv(2)
     second_stage(inputs, across)
     side_sent(*xs, d)
     side_done(inputs, down)
     fourth_stage(branch, across)
     fifth_stage(branch, d)
-    weight_qkv(2)
     fourth_stage(inputs, down)
+    side_sent(*cs, across)
     side_done(inputs, up)
-    weight_qkv(1)
-    side_sent(*cs, across)
+    weight_qkv(0)
+    fourth_stage(inputs, up)
+    weight_out(0)
     third_stage(inputs, across)
-    weight_qkv(0)
-    weight_out(0)
     weight_out(3)
     side_done(inputs, d)
-    fourth_stage(inputs, up)
+    weight_qkv(1)
     weight_qkv(5)
+    side_done(branch, down)
     side_sent(*cs, d)
     weight_qkv(3)
     side_done(inputs, across)
-    side_done(branch, down)
     fourth_stage(inputs, d)
     fourth_stage(inputs, across)
     weight_qkv(4)
+    fifth_stage(branch, across)
+    weight_out(2)
+    side_done(branch, across)
     first, second = stat_finish(stat_b)
     reciprocal = buf.recip[:, 0:1]
     centred = buf.centred[...]
@@ -916,6 +919,7 @@
     total = small_finish(gains)
     for part in range(2):
         hgg_ref[0, part] = total[2 * part : 2 * part + 2]
+    nb_ref[0] = last_stage(branch).astype(BF16)
     drain_gather(cot_ref.at[0], buf.big_c, cots)
     drain_gather(buf.norm, buf.big_x, acts)
     drain_depth(acts, 0, QKV)
@@ -923,10 +927,6 @@
     for step in range(4, 6):
         ring_copy(buf.att, cots, step).wait_send()
         ring_copy(buf.dp, acts, step).wait_send()
-    fifth_stage(branch, across)
-    side_done(branch, across)
-    weight_out(2)
-    nb_ref[0] = last_stage(branch).astype(BF16)
     drain_reduce(branch)
     drain_reduce(inputs)
     stat_drain(stat_a)

time: 189 us -> 185 us (0.979)
  Pallas kernels: 179 us -> 174 us
    pallas_call x1, Pallas kernels: 179 us -> 174 us  [local(): pl.pallas_call(kernel, out_shape=(jax.ShapeDtypeStruct((1, SEQ, FEATURES)...]
where the time goes in v4:
time: 185 us; the launch traced here: 183 us
  Pallas kernels  174 us (94%)
  local copies, waits for them, and re-layouts  8.74 us (5%)
    pallas_call x1, Pallas kernels, local(): pl.pallas_call(kernel, out_shape=(jax.ShapeDtypeStruct((1, SEQ, FEATURES)...  174 us
    reshape x1, local copies, waits for them, and re-layouts, local(): weight_grad.reshape(1, ROWS, 4, 256)  6.22 us

profile of v4, /device:TPU:32, one launch (start us, length us, event | category | flops | bytes accessed | tf_op | source)
XLA Modules:
  0.0 183.2 jit_solution(12518934772788644247)
XLA Ops:
  0.6 173.8 %block.1 = (bf16[1,256,384]{2,1,0:T(8,128)(2,1)}, bf16[1,256,384]{2,1,0:T(8,128)(2,1)}, bf16[1536,1024]{1,0:T(8,128)(2,1)}, f32[1,384]{1,0:T(1,128)}, f32[1,2,2,128]{3,2,1,0:T(2,128)}) custom-call(bf16[1,256,384]{2,1,0:T(8,128)(2,1)} %refs_0_.1, bf16[1,256,384]{2,1,0:T(8,128)(2,1)} %refs_1_.1, bf16[1,1536,4,256]{3,2,1,0:T(4,128)(2,1)} %refs_2_.1, ...), custom_call_target="tpu_custom_call" | custom-call | tf_op jit(solution)/shard_map/block/pallas_call | solution.py:944
  174.4 0.0 copy-start.1
  174.4 0.0 copy-start
  174.5 0.0 copy-start.3
  174.5 0.0 copy-start.2
  174.5 6.2 %reshape.13 = bf16[1,1536,4,256]{3,2,1,0:T(4,128)(2,1)} reshape(bf16[1536,1024]{1,0:T(8,128)(2,1)} %get-tuple-element.12) | data formatting | bytes 6291456 | tf_op jit(solution)/shard_map/reshape | solution.py:965
  180.7 0.0 copy-done.1
  180.7 0.7 copy.14
  181.4 0.0 copy-done
  181.4 0.7 copy.15
  182.1 0.0 copy-done.3
  182.1 0.6 copy.16
  182.6 0.0 copy-done.2
  182.6 0.6 copy.17
Async XLA Ops:
  174.4 6.3 %copy-start.1 = (bf16[1,256,384]{2,1,0:T(8,128)(2,1)S(1)}, bf16[1,256,384]{2,1,0:T(8,128)(2,1)}, u32[]{:S(2)}) copy-start(bf16[1,256,384]{2,1,0:T(8,128)(2,1)} %get-tuple-element.20) | copy-start | bytes 589828
  174.4 6.9 %copy-start = (bf16[1,256,384]{2,1,0:T(8,128)(2,1)S(1)}, bf16[1,256,384]{2,1,0:T(8,128)(2,1)}, u32[]{:S(2)}) copy-start(bf16[1,256,384]{2,1,0:T(8,128)(2,1)} %get-tuple-element.21) | copy-start | bytes 589828
  174.5 7.6 %copy-start.3 = (f32[1,384]{1,0:T(1,128)S(1)}, f32[1,384]{1,0:T(1,128)}, u32[]{:S(2)}) copy-start(f32[1,384]{1,0:T(1,128)} %get-tuple-element.23) | copy-start | bytes 4612
  174.5 8.2 %copy-start.2 = (f32[1,2,2,128]{3,2,1,0:T(2,128)S(1)}, f32[1,2,2,128]{3,2,1,0:T(2,128)}, u32[]{:S(2)}) copy-start(f32[1,2,2,128]{3,2,1,0:T(2,128)} %get-tuple-element.24) | copy-start | bytes 6148
